TPU v7x, 32 devices: a whole 2x2x4 slice. The times are simulated.
32 devices in a mesh: seq: 8 (over z, x), hid: 4 (over y, core).
Axes of the slice: x: 2, y: 2, z: 4, core: 2. Of those that a mesh axis runs over, the one named last changes fastest.
Arguments:
- tokens: bfloat16 [65536, 2048], P('seq', 'hid'), may hold values from -6 to 6
- cotangent: bfloat16 [65536, 2048], P('seq', 'hid'), may hold values from -6 to 6
- seq_first: bfloat16 [128, 512, 512], P('seq'), may hold values from -0.25 to 0.25
- seq_second: bfloat16 [512, 128, 128], P('seq'), may hold values from -0.5 to 0.5
- feat_first: bfloat16 [32, 64, 64], P('hid'), may hold values from -0.75 to 0.75
- feature_second_blocks: bfloat16 [64, 32, 32], P('hid'), may hold values from -1 to 1
- gate_scale: float32 [2048], P('hid'), may hold values from 0.5 to 2
- gate_bias: float32 [2048], P('hid'), may hold values from -3 to 3
Outputs:
- result: bfloat16 [65536, 2048], P('seq', 'hid')
- token_grad: bfloat16 [65536, 2048], P('seq', 'hid')
- first_grad: float32 [128, 512, 512], P('seq', 'hid')
- second_grad: float32 [512, 128, 128], P('seq', 'hid')
All inputs are finite; a program needn't handle non-finite values.
Results may differ from a plain program's by a relative error of at most 0.0061.
Values may be sent and summed in bfloat16 or wider, within the bound.
A program may use at most 256 MiB of HBM per device.

v0:
```python
import jax
import jax.numpy as jnp
from jax import lax
from jax.sharding import PartitionSpec as P


def gelu_slope(value):
    normal_cdf = 0.5 * (1.0 + jax.scipy.special.erf(value * 0.7071067811865476))
    density = jnp.exp(-0.5 * value * value) * 0.3989422804014327
    return normal_cdf + value * density


def to_strided(value):
    return lax.all_to_all(value, "seq", split_axis=1, concat_axis=0, tiled=True)


def from_strided(value):
    return lax.all_to_all(value, "seq", split_axis=0, concat_axis=1, tiled=True)


def feat_regroup(value):
    return lax.all_to_all(value, "hid", split_axis=1, concat_axis=0, tiled=True)


def feat_restore(value):
    return lax.all_to_all(value, "hid", split_axis=0, concat_axis=1, tiled=True)


def grad_sums(first_term, second_term):
    return (
        lax.psum_scatter(first_term, "hid", scatter_dimension=1, tiled=True),
        lax.psum_scatter(second_term, "hid", scatter_dimension=1, tiled=True),
    )


def on_device(
    tokens,
    cotangent,
    seq_first,
    seq_second,
    feat_first,
    feature_second_blocks,
    gate_scale,
    gate_bias,
):
    widened_input = jnp.float32
    half = jnp.bfloat16
    rows, width = tokens.shape
    blocks_here, block = (seq_first.shape[0], seq_first.shape[1])
    groups_here, group = (feat_first.shape[0], feat_first.shape[1])
    x_blocks = tokens.reshape(blocks_here, block, width)
    first = jnp.einsum(
        "qkj,qjc->qkc", seq_first, x_blocks, preferred_element_type=widened_input
    ).astype(half)
    strided = to_strided(first)
    mixed_strided = jnp.einsum(
        "jab,bjc->ajc", seq_second, strided, preferred_element_type=widened_input
    ).astype(half)
    mixed = from_strided(mixed_strided).reshape(rows, width).astype(widened_input)
    x_wide = tokens.astype(widened_input)
    gate = jax.nn.sigmoid(x_wide * gate_scale + gate_bias)
    hidden_state = (x_wide + gate * mixed).astype(half)
    panels = hidden_state.reshape(rows, groups_here, group)
    inner = jnp.einsum(
        "bio,tbo->bit", feat_first, panels, preferred_element_type=widened_input
    ).astype(half)
    cot_panels = cotangent.reshape(rows, groups_here, group).transpose(1, 2, 0)
    inner_moved = feat_regroup(inner)
    activation_values = jax.nn.gelu(inner_moved.astype(widened_input), approximate=False).astype(
        half
    )
    outer_shifted = jnp.einsum(
        "whg,gwv->hwv",
        feature_second_blocks,
        activation_values,
        preferred_element_type=widened_input,
    ).astype(half)
    outer = feat_restore(outer_shifted).transpose(2, 0, 1).reshape(rows, width)
    result = (hidden_state.astype(widened_input) + outer.astype(widened_input)).astype(half)
    cotangent_shifted = feat_regroup(cot_panels)
    activation_gradient = jnp.einsum(
        "hec,ehz->chz",
        feature_second_blocks,
        cotangent_shifted,
        preferred_element_type=widened_input,
    )
    d_inner = (activation_gradient * gelu_slope(inner_moved.astype(widened_input))).astype(half)
    d_back = feat_restore(d_inner)
    d_hidden = cotangent.astype(widened_input) + jnp.einsum(
        "bio,bit->tbo", feat_first, d_back, preferred_element_type=widened_input
    ).reshape(rows, width)
    d_mixed = (d_hidden * gate).astype(half).reshape(blocks_here, block, width)
    d_mixed_moved = to_strided(d_mixed)
    d_first_moved = jnp.einsum(
        "jab,ajc->bjc", seq_second, d_mixed_moved, preferred_element_type=widened_input
    ).astype(half)
    second_term = jnp.einsum(
        "ajc,bjc->jab", d_mixed_moved, strided, preferred_element_type=widened_input
    )
    d_first = from_strided(d_first_moved)
    local_part = d_hidden * (1.0 + gate_scale * gate * (1.0 - gate) * mixed)
    seq_part = jnp.einsum(
        "qkj,qkc->qjc", seq_first, d_first, preferred_element_type=widened_input
    ).reshape(rows, width)
    first_term = jnp.einsum("qkc,qjc->qkj", d_first, x_blocks, preferred_element_type=widened_input)
    first_grad, second_grad = grad_sums(first_term, second_term)
    token_grad = (seq_part + local_part).astype(half)
    return (result, token_grad, first_grad, second_grad)


def solution(mesh):
    return jax.shard_map(
        on_device,
        mesh=mesh,
        in_specs=(
            P("seq", "hid"),
            P("seq", "hid"),
            P("seq", None, None),
            P("seq", None, None),
            P("hid", None, None),
            P("hid", None, None),
            P("hid"),
            P("hid"),
        ),
        out_specs=(P("seq", "hid"), P("seq", "hid"), P("seq", "hid", None), P("seq", "hid", None)),
        check_vma=False,
    )
```

profile of v0, /device:TPU:0, one launch (start us, length us, event | category | flops | bytes accessed | tf_op | source)
XLA Modules:
  0.0 1590.5 jit_solution(16072981804615986163)
XLA Ops:
  7.2 13.8 convolution_convert_fusion.2
  21.0 11.5 copy.95
  32.5 190.6 %all_to_all.120 = bf16[16,512,512]{2,0,1:T(8,128)(2,1)} all-to-all(bf16[16,512,512]{2,0,1:T(8,128)(2,1)} %copy.95), channel_id=1, replica_groups=mesh['seq'=8,'hid'=4] {'seq'}, dimensions={1} | all-to-all | bytes 16777216 | tf_op jit(solution)/shard_map/all_to_all | solution.py:14
  223.1 11.9 copy.97
  235.0 15.5 convert_bitcast_fusion.3
  250.5 12.4 copy.99
  268.1 11.9 copy.107
  291.2 159.1 %all-to-all-done.1 = bf16[128,64,512]{2,1,0:T(8,128)(2,1)} async-done(((bf16[128,64,512]{2,1,0:T(8,128)(2,1)}), bf16[128,64,512]{2,1,0:T(8,128)(2,1)}, u32[]{:S(2)}, u32[]{:S(2)}) %all-to-all-start.1) | async-done | bytes 8388640 | tf_op jit(solution)/shard_map/all_to_all | solution.py:18
  455.9 11.7 convert_bitcast_fusion.1
  490.3 11.9 copy.101
  522.4 26.7 %all-to-all-done.4 = bf16[8,64,8192]{2,0,1:T(8,128)(2,1)} async-done(((bf16[8,64,8192]{2,0,1:T(8,128)(2,1)}), bf16[8,64,8192]{2,0,1:T(8,128)(2,1)}, u32[]{:S(2)}, u32[]{:S(2)}) %all-to-all-start.4) | async-done | bytes 8388640 | tf_op jit(solution)/shard_map/all_to_all | solution.py:22
  549.1 97.6 %all_to_all.121 = bf16[8,64,8192]{2,0,1:T(8,128)(2,1)S(1)} all-to-all(bf16[8,64,8192]{2,0,1:T(8,128)(2,1)} %copy.102), channel_id=1, replica_groups=mesh['seq'=8,'hid'=4] {'hid'}, dimensions={1} | all-to-all | bytes 16777216 | tf_op jit(solution)/shard_map/all_to_all | solution.py:22
  650.0 12.0 fusion.14
  673.1 100.7 %all_to_all.122 = bf16[32,16,8192]{2,1,0:T(8,128)(2,1)} all-to-all(bf16[32,16,8192]{2,1,0:T(8,128)(2,1)} %copy.112), channel_id=1, replica_groups=mesh['seq'=8,'hid'=4] {'hid'}, dimensions={0} | all-to-all | bytes 16777216 | tf_op jit(solution)/shard_map/all_to_all | solution.py:26
  781.5 11.5 fusion.78
  792.9 17.5 %copy.115 = f32[8192,512]{1,0:T(8,128)} copy(f32[8192,512]{0,1:T(8,128)} %bitcast.143) | data formatting | bytes 33554432 | tf_op jit(solution)/shard_map/reshape | solution.py:91
  810.4 15.5 multiply_convert_fusion
  837.2 188.7 %all_to_all.123 = bf16[16,512,512]{2,0,1:T(8,128)(2,1)} all-to-all(bf16[16,512,512]{2,0,1:T(8,128)(2,1)} %copy.116), channel_id=1, replica_groups=mesh['seq'=8,'hid'=4] {'seq'}, dimensions={1} | all-to-all | bytes 16777216 | tf_op jit(solution)/shard_map/all_to_all | solution.py:14
  1025.9 11.7 copy.118
  1037.6 16.9 %convert_bitcast_fusion.2 = bf16[128,64,512]{0,2,1:T(8,128)(2,1)} fusion(bf16[64,128,128]{2,1,0:T(8,128)(2,1)S(1)} %copy-done, bf16[128,64,512]{2,1,0:T(8,128)(2,1)} %bitcast.150), kind=kOutput, calls=%fused_computation.59 | convolution fusion | flops 1077936128 | bytes 18874368 | tf_op jit(solution)/shard_map/jab,ajc->bjc/dot_general | solution.py:94
  1054.6 12.6 copy.120
  1072.1 16.7 %fusion.39 = f32[64,128,128]{2,1,0:T(8,128)} fusion(bf16[128,64,512]{2,1,0:T(8,128)(2,1)} %bitcast.149, bf16[128,64,512]{2,1,0:T(8,128)(2,1)} %bitcast.151), kind=kOutput, calls=%fused_computation.63 | convolution fusion | flops 1073741824 | bytes 20971520 | tf_op jit(solution)/shard_map/ajc,bjc->jab/dot_general | solution.py:97
  1089.1 165.2 %all-to-all-done.7 = bf16[128,64,512]{2,1,0:T(8,128)(2,1)} async-done(((bf16[128,64,512]{2,1,0:T(8,128)(2,1)}), bf16[128,64,512]{2,1,0:T(8,128)(2,1)}, u32[]{:S(2)}, u32[]{:S(2)}) %all-to-all-start.7) | async-done | bytes 8388640 | tf_op jit(solution)/shard_map/all_to_all | solution.py:18
  1262.0 16.0 %fusion.80 = f32[16,512,512]{2,1,0:T(8,128)} fusion(bf16[16,512,512]{2,1,0:T(8,128)(2,1)} %bitcast.141, bf16[16,512,512]{2,1,0:T(8,128)(2,1)} %bitcast.138), kind=kOutput, calls=%fused_computation.101 | convolution fusion | flops 4294967296 | bytes 33554432 | tf_op jit(solution)/shard_map/qkc,qjc->qkj/dot_general | solution.py:105
  1278.1 39.5 %fusion.33 = bf16[32,16,8192]{2,0,1:T(8,128)(2,1)} fusion(bf16[16,32,32]{2,1,0:T(8,128)(2,1)S(1)} %copy-done.9, bf16[8,4,16,8192]{3,0,2,1:T(8,128)(2,1)} %bitcast.158), kind=kOutput, calls=%fused_computation.56 | convolution fusion | flops 549453824 | bytes 16809984 | tf_op jit(solution)/shard_map/whg,gwv->hwv/dot_general | solution.py:72
  1317.6 11.6 copy.104
  1329.2 162.1 %all_to_all.124 = bf16[32,16,8192]{2,1,0:T(8,128)(2,1)} all-to-all(bf16[32,16,8192]{2,1,0:T(8,128)(2,1)} %copy.104), channel_id=1, replica_groups=mesh['seq'=8,'hid'=4] {'hid'}, dimensions={0} | all-to-all | bytes 16777216 | tf_op jit(solution)/shard_map/all_to_all | solution.py:26
  1502.6 11.6 copy.105
  1514.2 17.5 %copy.106 = f32[8192,512]{1,0:T(8,128)} copy(f32[8192,512]{0,1:T(8,128)} %bitcast.144) | data formatting | bytes 33554432 | tf_op jit(solution)/shard_map/convert_element_type | solution.py:79
  1531.6 11.9 add_convert_fusion
  1543.5 13.1 fusion.79
  1556.6 26.8 %fusion.15 = bf16[8192,512]{1,0:T(8,128)(2,1)} fusion(f32[16,512,512]{1,2,0:T(8,128)} %fusion.79, f32[16,8,64,512]{3,2,1,0:T(8,128)} %copy-done.2, f32[8192,512]{1,0:T(8,128)} %copy.115, bf16[8192,512]{1,0:T(8,128)(2,1)} %param.9, f32[512]{0:T(512)S(1)} %copy-done.8, f32[512]{0:T(512)S(1)} %copy-done.6, bf16[8192,512]{1,0:T(8,128)(2,1)} %param.8), kind=kLoop, calls=%fused_computation.20 | loop fusion | flops 67108864 | bytes 75501568 | tf_op jit(solution)/shard_map/convert_element_type | solution.py:107
  (44 shorter events, 122.5 us)
Async XLA Ops:
  7.2 227.9 %copy-start = (bf16[64,128,128]{2,1,0:T(8,128)(2,1)S(1)}, bf16[64,128,128]{2,1,0:T(8,128)(2,1)}, u32[]{:S(2)}) copy-start(bf16[64,128,128]{2,1,0:T(8,128)(2,1)} %param.11) | copy-start | bytes 6291460
  262.9 187.4 %all-to-all-start.1 = ((bf16[128,64,512]{2,1,0:T(8,128)(2,1)}), bf16[128,64,512]{2,1,0:T(8,128)(2,1)}, u32[]{:S(2)}, u32[]{:S(2)}) async-start(bf16[128,64,512]{2,1,0:T(8,128)(2,1)} %copy.99), calls=%async_computation.1 | async-start | bytes 16777216 | tf_op jit(solution)/shard_map/all_to_all | solution.py:18
  450.3 98.8 %all-to-all-start.4 = ((bf16[8,64,8192]{2,0,1:T(8,128)(2,1)}), bf16[8,64,8192]{2,0,1:T(8,128)(2,1)}, u32[]{:S(2)}, u32[]{:S(2)}) async-start(bf16[8,64,8192]{2,0,1:T(8,128)(2,1)} %copy.108), calls=%async_computation.4 | async-start | bytes 16777216 | tf_op jit(solution)/shard_map/all_to_all | solution.py:22
  455.9 25.2 %slice-start = ((s8[8388608]{0:T(1024)(128)(4,1)}), s8[4194304]{0:T(1024)(128)(4,1)S(1)}, s32[]{:S(2)}) async-start(s8[8388608]{0:T(1024)(128)(4,1)} %bitcast.139), calls=%async_computation.12 | async-start | bytes 8388608
  467.7 13.5 slice-start.1
  467.7 13.5 copy-start.5
  467.7 13.5 copy-start.7
  475.4 5.7 copy-start.2
  490.3 11.9 copy-start.4
  511.2 138.8 %copy-start.9 = (bf16[16,32,32]{2,1,0:T(8,128)(2,1)S(1)}, bf16[16,32,32]{2,1,0:T(8,128)(2,1)}, u32[]{:S(2)}) copy-start(bf16[16,32,32]{2,1,0:T(8,128)(2,1)} %param.13) | copy-start | bytes 98308
  646.7 3.2 copy-start.3
  1067.1 187.2 %all-to-all-start.7 = ((bf16[128,64,512]{2,1,0:T(8,128)(2,1)}), bf16[128,64,512]{2,1,0:T(8,128)(2,1)}, u32[]{:S(2)}, u32[]{:S(2)}) async-start(bf16[128,64,512]{2,1,0:T(8,128)(2,1)} %copy.120), calls=%async_computation.7 | async-start | bytes 16777216 | tf_op jit(solution)/shard_map/all_to_all | solution.py:18
  1072.1 511.3 %reduce-scatter.5.cloned.1.call-start = ((), (), s32[]{:S(2)}) async-start(), calls=%async_computation.11 | async-start | bytes 5242880 | tf_op jit(solution)/shard_map/reduce_scatter | solution.py:32
  1088.9 494.5 %reduce-scatter.3.cloned.1.call-start = ((), (), s32[]{:S(2)}) async-start(), calls=%async_computation.10 | async-start | bytes 20971520 | tf_op jit(solution)/shard_map/reduce_scatter | solution.py:31
  1543.5 13.1 copy-start.6
  1543.5 13.1 copy-start.8
  1556.6 26.8 %copy-start.1 = (bf16[64,128,128]{2,1,0:T(8,128)(2,1)S(1)}, bf16[64,128,128]{2,1,0:T(8,128)(2,1)}, u32[]{:S(2)}) copy-start(bf16[64,128,128]{2,1,0:T(8,128)(2,1)} %param.11) | copy-start | bytes 6291460
Sparse Core Ops, SparseCore 0:
  1089.0 44.9 reduce-scatter.4
  1278.2 185.7 reduce-scatter.2
where the time goes:
time: 1600 us; the launch traced here: 1590 us
  blocking collectives  740 us (46%)
  waiting for transfers between devices  351 us (22%)
  local copies, waits for them, and re-layouts  219 us (14%)
  matrix products  164 us (10%)
  other arithmetic  86.4 us (5%)
  starting transfers between devices  16 us (1%)
    all_to_all x2, blocking collectives, to_strided(): return lax.all_to_all(value, 'seq', split_axis=1, concat_axis=0, tiled=True)  379 us
    all_to_all x2, waiting for transfers between devices, from_strided(): return lax.all_to_all(value, 'seq', split_axis=0, concat_axis=1, tiled=True)  324 us
    all_to_all x2, blocking collectives, feat_restore(): return lax.all_to_all(value, 'hid', split_axis=0, concat_axis=1, tiled=True)  263 us
    all_to_all x1, blocking collectives, feat_regroup(): return lax.all_to_all(value, 'hid', split_axis=1, concat_axis=0, tiled=True)  97.6 us
    dot_general x1, matrix products, on_device(): jnp.einsum('whg,gwv->hwv', feature_second_blocks, activation_values, pref...  39.5 us
  transfers between devices with their start and end apart: 5, of which 3 were waited for; matrix products, arithmetic and copies ran while one was open for 17% of the time, Pallas kernels for 0%

commit v1 on v0

v1 whole, which is shorter than its diff:
```python
import jax
import jax.numpy as jnp
from jax import lax
from jax.sharding import PartitionSpec as P

HALF = jnp.bfloat16
WIDE = jnp.float32


def dot(spec, left, right):
    return jnp.einsum(spec, left, right, preferred_element_type=WIDE)


def gelu_parts(value):
    normal_cdf = 0.5 * (1.0 + lax.erf(value * 0.7071067811865476))
    density = jnp.exp(-0.5 * value * value) * 0.3989422804014327
    return (value * normal_cdf).astype(HALF), normal_cdf + value * density


def swap_seq(value):
    return lax.all_to_all(value, "seq", split_axis=0, concat_axis=0, tiled=True)


def make_swap_hid(hid):
    pairwise = hid & (hid - 1) == 0 and hid <= 4

    def swap(value):
        lanes = value.shape[1] // hid
        if not pairwise:
            split = value.reshape(-1, hid, lanes).transpose(1, 0, 2)
            out = lax.all_to_all(split, "hid", split_axis=0, concat_axis=0, tiled=True)
            return out.transpose(1, 0, 2).reshape(value.shape)
        panels = [value[:, :lanes]]
        for step in range(1, hid):
            pairs = [(at, at ^ step) for at in range(hid)]
            panels.append(
                lax.ppermute(value[:, step * lanes : (step + 1) * lanes], "hid", pairs)
            )
        return jnp.concatenate(panels, axis=1)

    def order():
        at = jnp.arange(hid)
        return lax.axis_index("hid") ^ at if pairwise else at

    return swap, order


def on_device(seq, hid, tokens, cotangent, seq_first, seq_second, feat_first, feat_second, gate_scale, gate_bias):
    rows, width = tokens.shape
    blocks, block = seq_first.shape[:2]
    groups, group = feat_first.shape[:2]
    offsets_here, total_groups = feat_second.shape[:2]
    offsets = block // seq
    parts = 4 if offsets % 4 == 0 else 1
    step = offsets // parts
    part_rows = seq * blocks * step
    total_blocks = blocks * seq
    swap_hid, order = make_swap_hid(hid)
    panel = groups * offsets_here

    who = order()
    eye_b = jnp.eye(groups, dtype=HALF)
    w1 = feat_first.reshape(groups, hid, offsets_here, group)[:, who]
    into = jnp.einsum("bhio,bd->dohbi", w1, eye_b).reshape(width, hid * panel)
    back = into.T
    eye_i = jnp.eye(offsets_here, dtype=HALF)
    w2 = feat_second.reshape(offsets_here, hid, groups, hid, groups)[:, who][:, :, :, who]
    mix_out = jnp.einsum("ihbge,ij->gejhbi", w2, eye_i).reshape(hid * panel, hid * panel)
    mix_back = mix_out.T
    source = (
        jnp.arange(groups)[None, :, None] * group
        + who[:, None, None] * offsets_here
        + jnp.arange(offsets_here)[None, None, :]
    ).reshape(-1)
    spread = (source[:, None] == jnp.arange(width)[None, :]).astype(HALF)
    gather = spread.T

    def cut(value, length):
        return value.reshape(blocks, seq, parts, step, length)

    x_blocks = tokens.reshape(blocks, block, width)
    seq_rows = cut(seq_first, block)
    x_cut = cut(tokens, width)
    cot_cut = cut(cotangent, width)
    second_cut = seq_second.reshape(parts, step, total_blocks, total_blocks)

    def major(value):
        return value.transpose(1, 0, 2, 3).reshape(part_rows, width)

    weights = [seq_rows[:, :, p].reshape(blocks, seq * step, block) for p in range(parts)]
    strided, mixed, gates, hidden, inner = [], [], [], [], []
    for p in range(parts):
        first = dot("qkj,qjc->qkc", weights[p], x_blocks).astype(HALF)
        first = first.reshape(blocks, seq, step, width).transpose(1, 0, 2, 3)
        strided.append(swap_seq(first).reshape(total_blocks, step, width))
    for p in range(parts):
        here = dot("jab,bjc->ajc", second_cut[p], strided[p]).astype(HALF)
        mixed.append(swap_seq(here.reshape(seq, blocks, step, width)).reshape(part_rows, width))
    cots, cot_moved = [], []
    for p in range(parts):
        cots.append(major(cot_cut[:, :, p]))
        cot_moved.append(swap_hid(dot("tc,cd->td", cots[p], gather).astype(HALF)))
    results, moved, locals_, seconds = [], [], [], []
    for p in range(parts):
        x_wide = major(x_cut[:, :, p]).astype(WIDE)
        gate = jax.nn.sigmoid(x_wide * gate_scale + gate_bias)
        mixed_wide = mixed[p].astype(WIDE)
        state = (x_wide + gate * mixed_wide).astype(HALF)
        inner_moved = swap_hid(dot("tc,cd->td", state, into).astype(HALF))
        act, slope = gelu_parts(inner_moved.astype(WIDE))
        d_act = dot("td,ed->te", cot_moved[p], mix_out)
        d_inner = swap_hid((d_act * slope).astype(HALF))
        d_hidden = cots[p].astype(WIDE) + dot("td,dc->tc", d_inner, back)
        d_mixed = (d_hidden * gate).astype(HALF).reshape(seq, blocks, step, width)
        moved.append(swap_seq(d_mixed).reshape(total_blocks, step, width))
        locals_.append(
            (d_hidden * (1.0 + gate_scale * gate * (1.0 - gate) * mixed_wide)).astype(HALF)
        )
        outer = swap_hid(dot("td,de->te", act, mix_out).astype(HALF))
        outer = dot("td,dc->tc", outer, spread)
        results.append((state.astype(WIDE) + outer).astype(HALF))
    firsts, first_grads = [], []
    for p in range(parts):
        here = dot("jab,ajc->bjc", second_cut[p], moved[p]).astype(HALF)
        seconds.append(dot("ajc,bjc->jab", moved[p], strided[p]))
        back_here = swap_seq(here.reshape(seq, blocks, step, width))
        d_first = back_here.transpose(1, 0, 2, 3).reshape(blocks, seq * step, width)
        firsts.append(d_first)
        term = dot("qkc,qjc->qkj", d_first, x_blocks)
        term = lax.psum_scatter(term, "hid", scatter_dimension=1, tiled=True)
        first_grads.append(term.reshape(blocks, seq // hid, step, block))

    def join(values):
        stacked = jnp.stack([v.reshape(seq, blocks, step, width) for v in values])
        return stacked.transpose(2, 1, 0, 3, 4).reshape(rows, width)

    second_grad = lax.psum_scatter(
        jnp.concatenate(seconds, axis=0), "hid", scatter_dimension=1, tiled=True
    )
    seq_part = dot(
        "qkj,qkc->qjc", jnp.concatenate(weights, axis=1), jnp.concatenate(firsts, axis=1)
    ).reshape(rows, width)
    token_grad = (seq_part + join(locals_).astype(WIDE)).astype(HALF)
    first_grad = jnp.stack(first_grads, axis=2).reshape(blocks, block // hid, block)
    return (join(results), token_grad, first_grad, second_grad)


def solution(mesh):
    seq, hid = mesh.shape["seq"], mesh.shape["hid"]

    def body(*operands):
        return on_device(seq, hid, *operands)

    return jax.shard_map(
        body,
        mesh=mesh,
        in_specs=(
            P("seq", "hid"),
            P("seq", "hid"),
            P("seq", None, None),
            P("seq", None, None),
            P("hid", None, None),
            P("hid", None, None),
            P("hid"),
            P("hid"),
        ),
        out_specs=(P("seq", "hid"), P("seq", "hid"), P("seq", "hid", None), P("seq", "hid", None)),
        check_vma=False,
    )
```

time: 1600 us -> 1480 us (0.925)
  blocking collectives: 740 us -> 363 us
  waiting for transfers between devices: 351 us -> 535 us
  starting transfers between devices: 16 us -> 77.5 us
  local copies, waits for them, and re-layouts: 219 us -> 262 us
  other arithmetic: 86.4 us -> 61.5 us
    all_to_all x5 -> x7, blocking collectives: 740 us -> 363 us  [swap_seq(): return lax.all_to_all(value, 'seq', split_axis=0, concat_axis=0, tiled=True)]
    ppermute x0 -> x48, waiting for transfers between devices: none -> 218 us  [swap(): lax.ppermute(value[:, step * lanes:(step + 1) * lanes], 'hid', pairs)]
    convert_element_type x6 -> x8, other arithmetic: 86.4 us -> 46.7 us  [the longest x2 14.3 us: on_device(): token_grad = (seq_part + join(locals_).astype(WIDE)).astype(HALF)]
    ppermute x0 -> x48, starting transfers between devices: none -> 36.8 us  [swap(): lax.ppermute(value[:, step * lanes:(step + 1) * lanes], 'hid', pairs)]
    all_to_all x3 -> x9, waiting for transfers between devices: 351 us -> 316 us  [swap_seq(): return lax.all_to_all(value, 'seq', split_axis=0, concat_axis=0, tiled=True)]
    all_to_all x4 -> x8, local copies, waits for them, and re-layouts: 39 us -> 14.1 us  [swap_seq(): return lax.all_to_all(value, 'seq', split_axis=0, concat_axis=0, tiled=True)]
    all_to_all x3 -> x9, starting transfers between devices: 15.8 us -> 40.1 us  [swap_seq(): return lax.all_to_all(value, 'seq', split_axis=0, concat_axis=0, tiled=True)]
    slice x0 -> x17, local copies, waits for them, and re-layouts: none -> 21.2 us  [the longest x16 15.6 us: swap(): panels = [value[:, :lanes]]]
  transfers between devices with their start and end apart: 5 -> 62, of which waited for: 3 -> 31; matrix products, arithmetic and copies ran while one was open for 17% -> 28% of each run, Pallas kernels for 0% -> 0%
where the time goes in v1:
time: 1480 us; the launch traced here: 1470 us
  waiting for transfers between devices  535 us (36%)
  blocking collectives  363 us (25%)
  local copies, waits for them, and re-layouts  262 us (18%)
  matrix products  157 us (11%)
  starting transfers between devices  77.5 us (5%)
  other arithmetic  61.5 us (4%)
  between operations  15.5 us (1%)
    all_to_all x7, blocking collectives, swap_seq(): return lax.all_to_all(value, 'seq', split_axis=0, concat_axis=0, tiled=True)  363 us
    all_to_all x9, waiting for transfers between devices, swap_seq(): return lax.all_to_all(value, 'seq', split_axis=0, concat_axis=0, tiled=True)  316 us
    ppermute x48, waiting for transfers between devices, swap(): lax.ppermute(value[:, step * lanes:(step + 1) * lanes], 'hid', pairs)  218 us
    dot_general x45, matrix products, dot(): return jnp.einsum(spec, left, right, preferred_element_type=WIDE)  157 us
    convert_element_type x8, local copies, waits for them, and re-layouts, on_device(): x_wide = major(x_cut[:, :, p]).astype(WIDE)  41.5 us
    all_to_all x9, starting transfers between devices, swap_seq(): return lax.all_to_all(value, 'seq', split_axis=0, concat_axis=0, tiled=True)  40.1 us
    convert_element_type x8, local copies, waits for them, and re-layouts, on_device(): mixed_wide = mixed[p].astype(WIDE)  39.2 us
    ppermute x48, starting transfers between devices, swap(): lax.ppermute(value[:, step * lanes:(step + 1) * lanes], 'hid', pairs)  36.8 us
  transfers between devices with their start and end apart: 62, of which 31 were waited for; matrix products, arithmetic and copies ran while one was open for 28% of the time, Pallas kernels for 0%

profile of v1, /device:TPU:0, one launch (start us, length us, event | category | flops | bytes accessed | tf_op | source)
XLA Modules:
  0.0 1471.0 jit_solution(6113292565005290357)
XLA Ops:
  32.4 42.2 %all-to-all-done.6 = bf16[8,16,16,512]{3,2,1,0:T(8,128)(2,1)} async-done(((bf16[8,16,16,512]{3,2,1,0:T(8,128)(2,1)}), bf16[8,16,16,512]{3,2,1,0:T(8,128)(2,1)}, u32[]{:S(2)}, u32[]{:S(2)}) %all-to-all-start.6) | async-done | bytes 2097184 | tf_op jit(solution)/shard_map/all_to_all | solution.py:21
  85.1 41.7 %all-to-all-done = bf16[8,16,16,512]{3,2,1,0:T(8,128)(2,1)} async-done(((bf16[8,16,16,512]{3,2,1,0:T(8,128)(2,1)}), bf16[8,16,16,512]{3,2,1,0:T(8,128)(2,1)}, u32[]{:S(2)}, u32[]{:S(2)}) %all-to-all-start) | async-done | bytes 2097184 | tf_op jit(solution)/shard_map/all_to_all | solution.py:21
  137.3 41.6 %all-to-all-done.2 = bf16[8,16,16,512]{3,2,1,0:T(8,128)(2,1)} async-done(((bf16[8,16,16,512]{3,2,1,0:T(8,128)(2,1)}), bf16[8,16,16,512]{3,2,1,0:T(8,128)(2,1)}, u32[]{:S(2)}, u32[]{:S(2)}) %all-to-all-start.2) | async-done | bytes 2097184 | tf_op jit(solution)/shard_map/all_to_all | solution.py:21
  190.9 40.0 %all-to-all-done.4 = bf16[8,16,16,512]{3,2,1,0:T(8,128)(2,1)S(1)} async-done(((bf16[8,16,16,512]{3,2,1,0:T(8,128)(2,1)}), bf16[8,16,16,512]{3,2,1,0:T(8,128)(2,1)S(1)}, u32[]{:S(2)}, u32[]{:S(2)}) %all-to-all-start.4) | async-done | bytes 2097184 | tf_op jit(solution)/shard_map/all_to_all | solution.py:21
  244.6 39.9 %all-to-all-done.7 = bf16[8,16,16,512]{3,2,1,0:T(8,128)(2,1)S(1)} async-done(((bf16[8,16,16,512]{3,2,1,0:T(8,128)(2,1)}), bf16[8,16,16,512]{3,2,1,0:T(8,128)(2,1)S(1)}, u32[]{:S(2)}, u32[]{:S(2)}) %all-to-all-start.7) | async-done | bytes 2097184 | tf_op jit(solution)/shard_map/all_to_all | solution.py:21
  297.2 39.5 %all-to-all-done.1 = bf16[8,16,16,512]{3,2,1,0:T(8,128)(2,1)} async-done(((bf16[8,16,16,512]{3,2,1,0:T(8,128)(2,1)}), bf16[8,16,16,512]{3,2,1,0:T(8,128)(2,1)}, u32[]{:S(2)}, u32[]{:S(2)}) %all-to-all-start.1) | async-done | bytes 2097184 | tf_op jit(solution)/shard_map/all_to_all | solution.py:21
  361.1 27.7 %all-to-all-done.3 = bf16[8,16,16,512]{3,2,1,0:T(8,128)(2,1)} async-done(((bf16[8,16,16,512]{3,2,1,0:T(8,128)(2,1)}), bf16[8,16,16,512]{3,2,1,0:T(8,128)(2,1)}, u32[]{:S(2)}, u32[]{:S(2)}) %all-to-all-start.3) | async-done | bytes 2097184 | tf_op jit(solution)/shard_map/all_to_all | solution.py:21
  406.0 10.4 convert_bitcast_fusion.4
  493.9 8.9 add_convert_fusion.10
  584.5 10.2 collective-permute-done.14
  596.6 10.3 collective-permute-done.13
  629.2 11.4 collective-permute-done.7
  652.0 11.0 collective-permute-done.25
  664.6 8.8 collective-permute-done.2
  674.1 11.4 collective-permute-done.1
  696.6 11.4 collective-permute-done.46
  763.3 11.7 collective-permute-done.28
  776.6 19.1 %multiply_convert_fusion.7 = (bf16[2048,512]{0,1:T(8,128)(2,1)}, bf16[2048,512]{0,1:T(8,128)(2,1)}, bf16[2048,512]{0,1:T(8,128)(2,1)}, bf16[2048,512]{0,1:T(8,12...) fusion(f32[512]{0:T(512)S(1)} %copy-done.74, ...), kind=kOutput, calls=%fused_computation.94 | convolution fusion | flops 1142947840 | bytes 67637248 | tf_op jit(solution)/shard_map/td,dc->tc/dot_general | solution.py:11
  799.6 54.1 %all_to_all.80 = bf16[8,16,16,512]{3,2,1,0:T(8,128)(2,1)S(1)} all-to-all(bf16[8,16,16,512]{3,2,1,0:T(8,128)(2,1)} %bitcast.346), channel_id=1, replica_groups=mesh['seq'=8,'hid'=4] {'seq'}, dimensions={0} | all-to-all | bytes 4194304 | tf_op jit(solution)/shard_map/all_to_all | solution.py:21
  856.2 51.7 %all_to_all.81 = bf16[8,16,16,512]{3,1,2,0:T(8,128)(2,1)S(1)} all-to-all(bf16[8,16,16,512]{3,1,2,0:T(8,128)(2,1)S(1)} %copy.307), channel_id=1, replica_groups=mesh['seq'=8,'hid'=4] {'seq'}, dimensions={0} | all-to-all | bytes 4194304 | tf_op jit(solution)/shard_map/all_to_all | solution.py:21
  919.3 51.4 %all_to_all.82 = bf16[8,16,16,512]{3,2,1,0:T(8,128)(2,1)S(1)} all-to-all(bf16[8,16,16,512]{3,2,1,0:T(8,128)(2,1)} %bitcast.348), channel_id=1, replica_groups=mesh['seq'=8,'hid'=4] {'seq'}, dimensions={0} | all-to-all | bytes 4194304 | tf_op jit(solution)/shard_map/all_to_all | solution.py:21
  973.1 51.4 %all_to_all.83 = bf16[8,16,16,512]{3,1,2,0:T(8,128)(2,1)S(1)} all-to-all(bf16[8,16,16,512]{3,1,2,0:T(8,128)(2,1)S(1)} %copy.299), channel_id=1, replica_groups=mesh['seq'=8,'hid'=4] {'seq'}, dimensions={0} | all-to-all | bytes 4194304 | tf_op jit(solution)/shard_map/all_to_all | solution.py:21
  1036.0 51.3 %all_to_all.84 = bf16[8,16,16,512]{3,2,1,0:T(8,128)(2,1)S(1)} all-to-all(bf16[8,16,16,512]{3,2,1,0:T(8,128)(2,1)} %bitcast.350), channel_id=1, replica_groups=mesh['seq'=8,'hid'=4] {'seq'}, dimensions={0} | all-to-all | bytes 4194304 | tf_op jit(solution)/shard_map/all_to_all | solution.py:21
  1089.8 51.6 %all_to_all.85 = bf16[8,16,16,512]{3,1,2,0:T(8,128)(2,1)S(1)} all-to-all(bf16[8,16,16,512]{3,1,2,0:T(8,128)(2,1)S(1)} %copy.291), channel_id=1, replica_groups=mesh['seq'=8,'hid'=4] {'seq'}, dimensions={0} | all-to-all | bytes 4194304 | tf_op jit(solution)/shard_map/all_to_all | solution.py:21
  1152.7 51.4 %all_to_all.86 = bf16[8,16,16,512]{3,2,1,0:T(8,128)(2,1)S(1)} all-to-all(bf16[8,16,16,512]{3,2,1,0:T(8,128)(2,1)} %bitcast.352), channel_id=1, replica_groups=mesh['seq'=8,'hid'=4] {'seq'}, dimensions={0} | all-to-all | bytes 4194304 | tf_op jit(solution)/shard_map/all_to_all | solution.py:21
  1216.6 43.6 %all-to-all-done.9 = bf16[8,16,16,512]{3,1,2,0:T(8,128)(2,1)S(1)} async-done(((bf16[8,16,16,512]{3,1,2,0:T(8,128)(2,1)}), bf16[8,16,16,512]{3,1,2,0:T(8,128)(2,1)S(1)}, u32[]{:S(2)}, u32[]{:S(2)}) %all-to-all-start.9) | async-done | bytes 2097184 | tf_op jit(solution)/shard_map/all_to_all | solution.py:21
  1288.5 17.0 %collective-permute-done.22 = bf16[2048,128]{0,1:T(8,128)(2,1)S(1)} collective-permute-done((bf16[2048,128]{0,1:T(8,128)(2,1)S(1)}, bf16[2048,128]{0,1:T(8,128)(2,1)S(1)}, u32[]{:S(2)}, u32[]{:S(2)}) %collective-permute-start.22) | collective-permute-done | bytes 524320 | tf_op jit(solution)/shard_map/ppermute | solution.py:37
  1310.4 17.3 %collective-permute-done.17 = bf16[2048,128]{0,1:T(8,128)(2,1)S(1)} collective-permute-done((bf16[2048,128]{0,1:T(8,128)(2,1)S(1)}, bf16[2048,128]{0,1:T(8,128)(2,1)S(1)}, u32[]{:S(2)}, u32[]{:S(2)}) %collective-permute-start.17) | collective-permute-done | bytes 524320 | tf_op jit(solution)/shard_map/ppermute | solution.py:37
  1328.2 15.0 %collective-permute-done.16 = bf16[2048,128]{0,1:T(8,128)(2,1)S(1)} collective-permute-done((bf16[2048,128]{0,1:T(8,128)(2,1)S(1)}, bf16[2048,128]{0,1:T(8,128)(2,1)S(1)}, u32[]{:S(2)}, u32[]{:S(2)}) %collective-permute-start.16) | collective-permute-done | bytes 524320 | tf_op jit(solution)/shard_map/ppermute | solution.py:37
  1355.3 10.5 collective-permute-done.10
  1436.1 12.7 fusion.1
  1448.8 10.3 fusion
  (471 shorter events, 569.1 us)
Async XLA Ops:
  19.0 55.6 %all-to-all-start.6 = ((bf16[8,16,16,512]{3,2,1,0:T(8,128)(2,1)}), bf16[8,16,16,512]{3,2,1,0:T(8,128)(2,1)}, u32[]{:S(2)}, u32[]{:S(2)}) async-start(bf16[8,16,16,512]{3,2,1,0:T(8,128)(2,1)} %bitcast.341), calls=%async_computation.6 | async-start | bytes 4194304 | tf_op jit(solution)/shard_map/all_to_all | solution.py:21
  74.6 52.2 %all-to-all-start = ((bf16[8,16,16,512]{3,2,1,0:T(8,128)(2,1)}), bf16[8,16,16,512]{3,2,1,0:T(8,128)(2,1)}, u32[]{:S(2)}, u32[]{:S(2)}) async-start(bf16[8,16,16,512]{3,2,1,0:T(8,128)(2,1)} %bitcast.340), calls=%async_computation | async-start | bytes 4194304 | tf_op jit(solution)/shard_map/all_to_all | solution.py:21
  126.8 52.2 %all-to-all-start.2 = ((bf16[8,16,16,512]{3,2,1,0:T(8,128)(2,1)}), bf16[8,16,16,512]{3,2,1,0:T(8,128)(2,1)}, u32[]{:S(2)}, u32[]{:S(2)}) async-start(bf16[8,16,16,512]{3,2,1,0:T(8,128)(2,1)} %bitcast.339), calls=%async_computation.2 | async-start | bytes 4194304 | tf_op jit(solution)/shard_map/all_to_all | solution.py:21
  178.9 52.0 %all-to-all-start.4 = ((bf16[8,16,16,512]{3,2,1,0:T(8,128)(2,1)}), bf16[8,16,16,512]{3,2,1,0:T(8,128)(2,1)S(1)}, u32[]{:S(2)}, u32[]{:S(2)}) async-start(bf16[8,16,16,512]{3,2,1,0:T(8,128)(2,1)} %bitcast.338), calls=%async_computation.4 | async-start | bytes 4194304 | tf_op jit(solution)/shard_map/all_to_all | solution.py:21
  232.3 52.2 %all-to-all-start.7 = ((bf16[8,16,16,512]{3,2,1,0:T(8,128)(2,1)}), bf16[8,16,16,512]{3,2,1,0:T(8,128)(2,1)S(1)}, u32[]{:S(2)}, u32[]{:S(2)}) async-start(bf16[8,16,16,512]{3,2,1,0:T(8,128)(2,1)} %copy.268), calls=%async_computation.7 | async-start | bytes 4194304 | tf_op jit(solution)/shard_map/all_to_all | solution.py:21
  284.5 52.2 %all-to-all-start.1 = ((bf16[8,16,16,512]{3,2,1,0:T(8,128)(2,1)}), bf16[8,16,16,512]{3,2,1,0:T(8,128)(2,1)}, u32[]{:S(2)}, u32[]{:S(2)}) async-start(bf16[8,16,16,512]{3,2,1,0:T(8,128)(2,1)} %copy.225), calls=%async_computation.1 | async-start | bytes 4194304 | tf_op jit(solution)/shard_map/all_to_all | solution.py:21
  336.7 52.2 %all-to-all-start.3 = ((bf16[8,16,16,512]{3,2,1,0:T(8,128)(2,1)}), bf16[8,16,16,512]{3,2,1,0:T(8,128)(2,1)}, u32[]{:S(2)}, u32[]{:S(2)}) async-start(bf16[8,16,16,512]{3,2,1,0:T(8,128)(2,1)} %copy.241), calls=%async_computation.3 | async-start | bytes 4194304 | tf_op jit(solution)/shard_map/all_to_all | solution.py:21
  349.7 176.0 %collective-permute-start.44 = (bf16[2048,128]{0,1:T(8,128)(2,1)}, bf16[2048,128]{0,1:T(8,128)(2,1)}, u32[]{:S(2)}, u32[]{:S(2)}) collective-permute-start(bf16[2048,128]{0,1:T(8,128)(2,1)} %get-tuple-element.57), channel_id=1, source_target_pairs={{0,3},{1,2},{2,1},{3,0},{4,7},{5,6},{6,5},{7,4},{8,11},{9,10},{10,... | collective-permute-start | bytes 1572872 | tf_op jit(solution)/shard_map/ppermute | solution.py:37
  349.8 177.4 %collective-permute-start.43 = (bf16[2048,128]{0,1:T(8,128)(2,1)}, bf16[2048,128]{0,1:T(8,128)(2,1)}, u32[]{:S(2)}, u32[]{:S(2)}) collective-permute-start(bf16[2048,128]{0,1:T(8,128)(2,1)} %get-tuple-element.58), channel_id=1, source_target_pairs={{0,2},{1,3},{2,0},{3,1},{4,6},{5,7},{6,4},{7,5},{8,10},{9,11},{10,... | collective-permute-start | bytes 1572872 | tf_op jit(solution)/shard_map/ppermute | solution.py:37
  351.2 176.4 %collective-permute-start.42 = (bf16[2048,128]{0,1:T(8,128)(2,1)}, bf16[2048,128]{0,1:T(8,128)(2,1)}, u32[]{:S(2)}, u32[]{:S(2)}) collective-permute-start(bf16[2048,128]{0,1:T(8,128)(2,1)} %get-tuple-element.59), channel_id=1, source_target_pairs={{0,1},{1,0},{2,3},{3,2},{4,5},{5,4},{6,7},{7,6},{8,9},{9,8},{10,11... | collective-permute-start | bytes 1572872 | tf_op jit(solution)/shard_map/ppermute | solution.py:37
  388.9 105.0 %all-to-all-start.5 = ((bf16[8,16,16,512]{3,2,1,0:T(8,128)(2,1)}), bf16[8,16,16,512]{3,2,1,0:T(8,128)(2,1)}, u32[]{:S(2)}, u32[]{:S(2)}) async-start(bf16[8,16,16,512]{3,2,1,0:T(8,128)(2,1)} %copy.255), calls=%async_computation.5 | async-start | bytes 4194304 | tf_op jit(solution)/shard_map/all_to_all | solution.py:21
  393.2 1065.9 %reduce-scatter.12.cloned.1.call-start = ((), (), s32[]{:S(2)}) async-start(), calls=%async_computation.24 | async-start | bytes 5242880 | tf_op jit(solution)/shard_map/reduce_scatter | solution.py:130
  396.6 171.8 %collective-permute-start.38 = (bf16[2048,128]{0,1:T(8,128)(2,1)}, bf16[2048,128]{0,1:T(8,128)(2,1)}, u32[]{:S(2)}, u32[]{:S(2)}) collective-permute-start(bf16[2048,128]{0,1:T(8,128)(2,1)} %get-tuple-element.49), channel_id=1, source_target_pairs={{0,3},{1,2},{2,1},{3,0},{4,7},{5,6},{6,5},{7,4},{8,11},{9,10},{10,... | collective-permute-start | bytes 1572872 | tf_op jit(solution)/shard_map/ppermute | solution.py:37
  396.7 173.0 %collective-permute-start.37 = (bf16[2048,128]{0,1:T(8,128)(2,1)}, bf16[2048,128]{0,1:T(8,128)(2,1)}, u32[]{:S(2)}, u32[]{:S(2)}) collective-permute-start(bf16[2048,128]{0,1:T(8,128)(2,1)} %get-tuple-element.50), channel_id=1, source_target_pairs={{0,2},{1,3},{2,0},{3,1},{4,6},{5,7},{6,4},{7,5},{8,10},{9,11},{10,... | collective-permute-start | bytes 1572872 | tf_op jit(solution)/shard_map/ppermute | solution.py:37
  525.7 45.5 %collective-permute-start.20 = (bf16[2048,128]{0,1:T(8,128)(2,1)}, bf16[2048,128]{0,1:T(8,128)(2,1)}, u32[]{:S(2)}, u32[]{:S(2)}) collective-permute-start(bf16[2048,128]{0,1:T(8,128)(2,1)} %get-tuple-element.89), channel_id=1, source_target_pairs={{0,3},{1,2},{2,1},{3,0},{4,7},{5,6},{6,5},{7,4},{8,11},{9,10},{10,... | collective-permute-start | bytes 1572872 | tf_op jit(solution)/shard_map/ppermute | solution.py:37
  527.1 44.4 %collective-permute-start.19 = (bf16[2048,128]{0,1:T(8,128)(2,1)}, bf16[2048,128]{0,1:T(8,128)(2,1)}, u32[]{:S(2)}, u32[]{:S(2)}) collective-permute-start(bf16[2048,128]{0,1:T(8,128)(2,1)} %get-tuple-element.90), channel_id=1, source_target_pairs={{0,2},{1,3},{2,0},{3,1},{4,6},{5,7},{6,4},{7,5},{8,10},{9,11},{10,... | collective-permute-start | bytes 1572872 | tf_op jit(solution)/shard_map/ppermute | solution.py:37
  527.6 45.4 %collective-permute-start.18 = (bf16[2048,128]{0,1:T(8,128)(2,1)}, bf16[2048,128]{0,1:T(8,128)(2,1)}, u32[]{:S(2)}, u32[]{:S(2)}) collective-permute-start(bf16[2048,128]{0,1:T(8,128)(2,1)} %get-tuple-element.91), channel_id=1, source_target_pairs={{0,1},{1,0},{2,3},{3,2},{4,5},{5,4},{6,7},{7,6},{8,9},{9,8},{10,11... | collective-permute-start | bytes 1572872 | tf_op jit(solution)/shard_map/ppermute | solution.py:37
  618.5 44.6 %collective-permute-start.25 = (bf16[2048,128]{0,1:T(8,128)(2,1)S(1)}, bf16[2048,128]{0,1:T(8,128)(2,1)S(1)}, u32[]{:S(2)}, u32[]{:S(2)}) collective-permute-start(bf16[2048,128]{0,1:T(8,128)(2,1)S(1)} %copy-done.56), channel_id=1, source_target_pairs={{0,2},{1,3},{2,0},{3,1},{4,6},{5,7},{6,4},{7,5},{8,10},{9,11},{10,... | collective-permute-start | bytes 1572872 | tf_op jit(solution)/shard_map/ppermute | solution.py:37
  640.9 44.6 %collective-permute-start.1 = (bf16[2048,128]{0,1:T(8,128)(2,1)S(1)}, bf16[2048,128]{0,1:T(8,128)(2,1)S(1)}, u32[]{:S(2)}, u32[]{:S(2)}) collective-permute-start(bf16[2048,128]{0,1:T(8,128)(2,1)S(1)} %get-tuple-element.66), channel_id=1, source_target_pairs={{0,2},{1,3},{2,0},{3,1},{4,6},{5,7},{6,4},{7,5},{8,10},{9,11},{10,... | collective-permute-start | bytes 1572872 | tf_op jit(solution)/shard_map/ppermute | solution.py:37
  663.4 44.6 %collective-permute-start.46 = (bf16[2048,128]{0,1:T(8,128)(2,1)S(1)}, bf16[2048,128]{0,1:T(8,128)(2,1)S(1)}, u32[]{:S(2)}, u32[]{:S(2)}) collective-permute-start(bf16[2048,128]{0,1:T(8,128)(2,1)S(1)} %get-tuple-element.54), channel_id=1, source_target_pairs={{0,2},{1,3},{2,0},{3,1},{4,6},{5,7},{6,4},{7,5},{8,10},{9,11},{10,... | collective-permute-start | bytes 1572872 | tf_op jit(solution)/shard_map/ppermute | solution.py:37
  685.9 44.6 %collective-permute-start.40 = (bf16[2048,128]{0,1:T(8,128)(2,1)S(1)}, bf16[2048,128]{0,1:T(8,128)(2,1)S(1)}, u32[]{:S(2)}, u32[]{:S(2)}) collective-permute-start(bf16[2048,128]{0,1:T(8,128)(2,1)S(1)} %get-tuple-element.46), channel_id=1, source_target_pairs={{0,2},{1,3},{2,0},{3,1},{4,6},{5,7},{6,4},{7,5},{8,10},{9,11},{10,... | collective-permute-start | bytes 1572872 | tf_op jit(solution)/shard_map/ppermute | solution.py:37
  730.8 44.1 %collective-permute-start.28 = (bf16[2048,128]{0,1:T(8,128)(2,1)S(1)}, bf16[2048,128]{0,1:T(8,128)(2,1)S(1)}, u32[]{:S(2)}, u32[]{:S(2)}) collective-permute-start(bf16[2048,128]{0,1:T(8,128)(2,1)S(1)} %get-tuple-element.30), channel_id=1, source_target_pairs={{0,2},{1,3},{2,0},{3,1},{4,6},{5,7},{6,4},{7,5},{8,10},{9,11},{10,... | collective-permute-start | bytes 1572872 | tf_op jit(solution)/shard_map/ppermute | solution.py:37
  915.3 543.8 %reduce-scatter.10.cloned.1.call-start = ((), (), s32[]{:S(2)}) async-start(), calls=%async_computation.23 | async-start | bytes 5242880 | tf_op jit(solution)/shard_map/reduce_scatter | solution.py:130
  1032.0 427.1 %reduce-scatter.8.cloned.1.call-start = ((), (), s32[]{:S(2)}) async-start(), calls=%async_computation.22 | async-start | bytes 5242880 | tf_op jit(solution)/shard_map/reduce_scatter | solution.py:130
  1209.0 51.3 %all-to-all-start.9 = ((bf16[8,16,16,512]{3,1,2,0:T(8,128)(2,1)}), bf16[8,16,16,512]{3,1,2,0:T(8,128)(2,1)S(1)}, u32[]{:S(2)}, u32[]{:S(2)}) async-start(bf16[8,16,16,512]{3,1,2,0:T(8,128)(2,1)} %copy.283), calls=%async_computation.9 | async-start | bytes 4194304 | tf_op jit(solution)/shard_map/all_to_all | solution.py:21
  1212.6 246.6 %reduce-scatter.6.cloned.1.call-start = ((), (), s32[]{:S(2)}) async-start(), calls=%async_computation.21 | async-start | bytes 5242880 | tf_op jit(solution)/shard_map/reduce_scatter | solution.py:130
  1271.0 193.3 %reduce-scatter.14.cloned.1.call-start = ((), (), s32[]{:S(2)}) async-start(), calls=%async_computation.25 | async-start | bytes 5242880 | tf_op jit(solution)/shard_map/reduce_scatter | solution.py:137
  1278.4 49.3 %collective-permute-start.17 = (bf16[2048,128]{0,1:T(8,128)(2,1)S(1)}, bf16[2048,128]{0,1:T(8,128)(2,1)S(1)}, u32[]{:S(2)}, u32[]{:S(2)}) collective-permute-start(bf16[2048,128]{0,1:T(8,128)(2,1)S(1)} %get-tuple-element.77), channel_id=1, source_target_pairs={{0,3},{1,2},{2,1},{3,0},{4,7},{5,6},{6,5},{7,4},{8,11},{9,10},{10,... | collective-permute-start | bytes 1572872 | tf_op jit(solution)/shard_map/ppermute | solution.py:37
  1279.5 63.7 %collective-permute-start.16 = (bf16[2048,128]{0,1:T(8,128)(2,1)S(1)}, bf16[2048,128]{0,1:T(8,128)(2,1)S(1)}, u32[]{:S(2)}, u32[]{:S(2)}) collective-permute-start(bf16[2048,128]{0,1:T(8,128)(2,1)S(1)} %get-tuple-element.78), channel_id=1, source_target_pairs={{0,2},{1,3},{2,0},{3,1},{4,6},{5,7},{6,4},{7,5},{8,10},{9,11},{10,... | collective-permute-start | bytes 1572872 | tf_op jit(solution)/shard_map/ppermute | solution.py:37
  1288.4 55.7 %collective-permute-start.15 = (bf16[2048,128]{0,1:T(8,128)(2,1)S(1)}, bf16[2048,128]{0,1:T(8,128)(2,1)S(1)}, u32[]{:S(2)}, u32[]{:S(2)}) collective-permute-start(bf16[2048,128]{0,1:T(8,128)(2,1)S(1)} %get-tuple-element.79), channel_id=1, source_target_pairs={{0,1},{1,0},{2,3},{3,2},{4,5},{5,4},{6,7},{7,6},{8,9},{9,8},{10,11... | collective-permute-start | bytes 1572872 | tf_op jit(solution)/shard_map/ppermute | solution.py:37
  1305.6 49.5 %collective-permute-start.11 = (bf16[2048,128]{0,1:T(8,128)(2,1)}, bf16[2048,128]{0,1:T(8,128)(2,1)}, u32[]{:S(2)}, u32[]{:S(2)}) collective-permute-start(bf16[2048,128]{0,1:T(8,128)(2,1)} %get-tuple-element.69), channel_id=1, source_target_pairs={{0,3},{1,2},{2,1},{3,0},{4,7},{5,6},{6,5},{7,4},{8,11},{9,10},{10,... | collective-permute-start | bytes 1572872 | tf_op jit(solution)/shard_map/ppermute | solution.py:37
  1307.9 57.9 %collective-permute-start.10 = (bf16[2048,128]{0,1:T(8,128)(2,1)}, bf16[2048,128]{0,1:T(8,128)(2,1)}, u32[]{:S(2)}, u32[]{:S(2)}) collective-permute-start(bf16[2048,128]{0,1:T(8,128)(2,1)} %get-tuple-element.70), channel_id=1, source_target_pairs={{0,2},{1,3},{2,0},{3,1},{4,6},{5,7},{6,4},{7,5},{8,10},{9,11},{10,... | collective-permute-start | bytes 1572872 | tf_op jit(solution)/shard_map/ppermute | solution.py:37
  (132 other events, 3061.4 us)
Sparse Core Ops, SparseCore 0:
  915.4 43.4 reduce-scatter.11
  1032.1 43.4 reduce-scatter.9
  1148.9 43.4 reduce-scatter.7
  1271.1 66.1 reduce-scatter.5
  1386.7 43.7 reduce-scatter.13

commit v2 on v1

--- a/solution.py
+++ b/solution.py
@@ -1,6 +1,7 @@
 import jax
 import jax.numpy as jnp
 from jax import lax
+from jax.experimental.layout import Layout, with_layout_constraint
 from jax.sharding import PartitionSpec as P
 
 HALF = jnp.bfloat16
@@ -15,6 +16,10 @@
     normal_cdf = 0.5 * (1.0 + lax.erf(value * 0.7071067811865476))
     density = jnp.exp(-0.5 * value * value) * 0.3989422804014327
     return (value * normal_cdf).astype(HALF), normal_cdf + value * density
+
+
+def rowwise(value):
+    return with_layout_constraint(value, Layout(major_to_minor=(0, 1)))
 
 
 def swap_seq(value):
@@ -88,47 +93,121 @@
         return value.transpose(1, 0, 2, 3).reshape(part_rows, width)
 
     weights = [seq_rows[:, :, p].reshape(blocks, seq * step, block) for p in range(parts)]
-    strided, mixed, gates, hidden, inner = [], [], [], [], []
-    for p in range(parts):
-        first = dot("qkj,qjc->qkc", weights[p], x_blocks).astype(HALF)
-        first = first.reshape(blocks, seq, step, width).transpose(1, 0, 2, 3)
-        strided.append(swap_seq(first).reshape(total_blocks, step, width))
-    for p in range(parts):
-        here = dot("jab,bjc->ajc", second_cut[p], strided[p]).astype(HALF)
-        mixed.append(swap_seq(here.reshape(seq, blocks, step, width)).reshape(part_rows, width))
-    cots, cot_moved = [], []
-    for p in range(parts):
-        cots.append(major(cot_cut[:, :, p]))
-        cot_moved.append(swap_hid(dot("tc,cd->td", cots[p], gather).astype(HALF)))
-    results, moved, locals_, seconds = [], [], [], []
-    for p in range(parts):
-        x_wide = major(x_cut[:, :, p]).astype(WIDE)
-        gate = jax.nn.sigmoid(x_wide * gate_scale + gate_bias)
-        mixed_wide = mixed[p].astype(WIDE)
-        state = (x_wide + gate * mixed_wide).astype(HALF)
-        inner_moved = swap_hid(dot("tc,cd->td", state, into).astype(HALF))
-        act, slope = gelu_parts(inner_moved.astype(WIDE))
-        d_act = dot("td,ed->te", cot_moved[p], mix_out)
-        d_inner = swap_hid((d_act * slope).astype(HALF))
-        d_hidden = cots[p].astype(WIDE) + dot("td,dc->tc", d_inner, back)
-        d_mixed = (d_hidden * gate).astype(HALF).reshape(seq, blocks, step, width)
-        moved.append(swap_seq(d_mixed).reshape(total_blocks, step, width))
-        locals_.append(
-            (d_hidden * (1.0 + gate_scale * gate * (1.0 - gate) * mixed_wide)).astype(HALF)
-        )
-        outer = swap_hid(dot("td,de->te", act, mix_out).astype(HALF))
-        outer = dot("td,dc->tc", outer, spread)
-        results.append((state.astype(WIDE) + outer).astype(HALF))
-    firsts, first_grads = [], []
-    for p in range(parts):
-        here = dot("jab,ajc->bjc", second_cut[p], moved[p]).astype(HALF)
-        seconds.append(dot("ajc,bjc->jab", moved[p], strided[p]))
-        back_here = swap_seq(here.reshape(seq, blocks, step, width))
-        d_first = back_here.transpose(1, 0, 2, 3).reshape(blocks, seq * step, width)
-        firsts.append(d_first)
+    sent = (seq, blocks, step, width)
+    everyone = range(parts)
+    held = {}
+
+    def first_of(p):
+        first = dot("qkj,qjc->qkc", weights[p], held["x"]).astype(HALF)
+        held["send1", p] = first.reshape(blocks, seq, step, width).transpose(1, 0, 2, 3)
+
+    def cot_of(p):
+        held["cot", p] = rowwise(major(cot_cut[:, :, p]))
+        panels = rowwise(dot("tc,cd->td", held["cot", p], gather).astype(HALF))
+        held["cot_moved", p] = swap_hid(panels)
+
+    def mix_of(p):
+        strided = held["strided", p].reshape(total_blocks, step, width)
+        here = dot("jab,bjc->ajc", second_cut[p], strided).astype(HALF)
+        held["send2", p] = here.reshape(sent)
+
+    def gate_of(p):
+        x_wide = held["x", p].astype(WIDE)
+        return x_wide, jax.nn.sigmoid(x_wide * gate_scale + gate_bias)
+
+    def inner_of(p):
+        held["x", p] = rowwise(major(x_cut[:, :, p]))
+        x_wide, gate = gate_of(p)
+        mixed_wide = rowwise(held["mixed", p].reshape(part_rows, width)).astype(WIDE)
+        state = rowwise((x_wide + gate * mixed_wide).astype(HALF))
+        held["state", p] = state
+        panels = rowwise(dot("tc,cd->td", state, into).astype(HALF))
+        held["inner", p] = swap_hid(panels)
+
+    def d_inner_of(p):
+        act, slope = gelu_parts(held["inner", p].astype(WIDE))
+        held["act", p] = rowwise(act)
+        d_act = dot("td,ed->te", held["cot_moved", p], mix_out)
+        held["d_inner", p] = swap_hid(rowwise((d_act * slope).astype(HALF)))
+
+    def d_mixed_of(p):
+        d_hidden = held["cot", p].astype(WIDE) + dot("td,dc->tc", held["d_inner", p], back)
+        x_wide, gate = gate_of(p)
+        mixed_wide = held["mixed", p].reshape(part_rows, width).astype(WIDE)
+        held["send3", p] = rowwise((d_hidden * gate).astype(HALF)).reshape(sent)
+        local = d_hidden * (1.0 + gate_scale * gate * (1.0 - gate) * mixed_wide)
+        held["local", p] = rowwise(local.astype(HALF))
+
+    def result_of(p):
+        panels = rowwise(dot("td,de->te", held["act", p], mix_out).astype(HALF))
+        outer = dot("td,dc->tc", swap_hid(panels), spread)
+        held["result", p] = rowwise((held["state", p].astype(WIDE) + outer).astype(HALF))
+
+    def d_first_of(p):
+        moved = held["moved", p].reshape(total_blocks, step, width)
+        here = dot("jab,ajc->bjc", second_cut[p], moved).astype(HALF)
+        held["send4", p] = here.reshape(sent)
+        strided = held["strided", p].reshape(total_blocks, step, width)
+        held["second", p] = dot("ajc,bjc->jab", moved, strided)
+
+    def term_of(p):
+        d_first = held["back", p].transpose(1, 0, 2, 3).reshape(blocks, seq * step, width)
+        held["d_first", p] = d_first
         term = dot("qkc,qjc->qkj", d_first, x_blocks)
         term = lax.psum_scatter(term, "hid", scatter_dimension=1, tiled=True)
-        first_grads.append(term.reshape(blocks, seq // hid, step, block))
+        held["grad", p] = term.reshape(blocks, seq // hid, step, block)
+
+    moves = [
+        (name, p)
+        for name in (("send1", "strided"), ("send2", "mixed"), ("send3", "moved"), ("send4", "back"))
+        for p in everyone
+    ]
+    plan = {n: [] for n in range(len(moves) + 1)}
+    for p in everyone:
+        if p:
+            plan[p - 1].append((first_of, p))
+        plan[p].append((cot_of, p))
+        plan[parts if p == parts - 1 else p + 1].append((mix_of, p))
+        after = parts + p
+        plan[after + 1].append((inner_of, p))
+        plan[after + 2].append((d_inner_of, p))
+        plan[after + (3 if parts > 3 else 2)].append((d_mixed_of, p))
+        plan[2 * parts + p + 1].append((d_first_of, p))
+        plan[2 * parts + p + 2].append((result_of, p))
+        plan[3 * parts + p + 1].append((term_of, p))
+    held["x"] = x_blocks
+    first_of(0)
+    if parts == 1:
+        held["strided", 0] = swap_seq(held["send1", 0])
+        cot_of(0)
+        mix_of(0)
+        held["mixed", 0] = swap_seq(held["send2", 0])
+        inner_of(0)
+        d_inner_of(0)
+        d_mixed_of(0)
+        result_of(0)
+        held["moved", 0] = swap_seq(held["send3", 0])
+        d_first_of(0)
+        held["back", 0] = swap_seq(held["send4", 0])
+        term_of(0)
+    else:
+        for n, ((source_name, target), p) in enumerate(moves):
+            names = [k for k in held if k[0] not in ("grad", "second")]
+            for name, value in zip(names, lax.optimization_barrier([held[k] for k in names])):
+                held[name] = value
+            arrived = swap_seq(held[source_name, p])
+            for work, q in plan[n]:
+                work(q)
+            held[target, p] = arrived
+            del held[source_name, p]
+        for work, q in plan[len(moves)]:
+            work(q)
+
+    firsts = [held["d_first", p] for p in everyone]
+    first_grads = [held["grad", p] for p in everyone]
+    seconds = [held["second", p] for p in everyone]
+    locals_ = [held["local", p] for p in everyone]
+    results = [held["result", p] for p in everyone]
 
     def join(values):
         stacked = jnp.stack([v.reshape(seq, blocks, step, width) for v in values])

time: 1480 us -> 1060 us (0.72)
  blocking collectives: 363 us -> 106 us
  local copies, waits for them, and re-layouts: 262 us -> 129 us
  waiting for transfers between devices: 535 us -> 466 us
  starting transfers between devices: 77.5 us -> 104 us
    all_to_all x7 -> x2, blocking collectives: 363 us -> 106 us  [swap_seq(): return lax.all_to_all(value, 'seq', split_axis=0, concat_axis=0, tiled=True)]
    all_to_all x9 -> x14, waiting for transfers between devices: 316 us -> 173 us  [swap_seq(): return lax.all_to_all(value, 'seq', split_axis=0, concat_axis=0, tiled=True)]
    convert_element_type x32 -> x0, local copies, waits for them, and re-layouts: 127 us -> none  [the longest x8 41.5 us: on_device(): x_wide = major(x_cut[:, :, p]).astype(WIDE)]
    ppermute x48, waiting for transfers between devices: 218 us -> 269 us  [swap(): lax.ppermute(value[:, step * lanes:(step + 1) * lanes], 'hid', pairs)]
    optimization_barrier x0 -> x12, local copies, waits for them, and re-layouts: none -> 33.4 us  [on_device(): lax.optimization_barrier([held[k] for k in names])]
    all_to_all x9 -> x14, starting transfers between devices: 40.1 us -> 68.4 us  [swap_seq(): return lax.all_to_all(value, 'seq', split_axis=0, concat_axis=0, tiled=True)]
    reshape x16 -> x4, local copies, waits for them, and re-layouts: 34.4 us -> 6.04 us  [first_of(): first.reshape(blocks, seq, step, width).transpose(1, 0, 2, 3)]
    reduce_scatter x1, waiting for transfers between devices: 0.01 us -> 23.8 us  [on_device(): lax.psum_scatter(jnp.concatenate(seconds, axis=0), 'hid', scatter_dimensi...]
  transfers between devices with their start and end apart: 62 -> 67, of which waited for: 31 -> 41; matrix products, arithmetic and copies ran while one was open for 28% -> 28% of each run, Pallas kernels for 0% -> 0%
where the time goes in v2:
time: 1060 us; the launch traced here: 1050 us
  waiting for transfers between devices  466 us (44%)
  matrix products  166 us (16%)
  local copies, waits for them, and re-layouts  129 us (12%)
  blocking collectives  106 us (10%)
  starting transfers between devices  104 us (10%)
  other arithmetic  65.4 us (6%)
  between operations  15.3 us (1%)
    ppermute x48, waiting for transfers between devices, swap(): lax.ppermute(value[:, step * lanes:(step + 1) * lanes], 'hid', pairs)  269 us
    all_to_all x14, waiting for transfers between devices, swap_seq(): return lax.all_to_all(value, 'seq', split_axis=0, concat_axis=0, tiled=True)  173 us
    dot_general x45, matrix products, dot(): return jnp.einsum(spec, left, right, preferred_element_type=WIDE)  166 us
    all_to_all x2, blocking collectives, swap_seq(): return lax.all_to_all(value, 'seq', split_axis=0, concat_axis=0, tiled=True)  106 us
    all_to_all x14, starting transfers between devices, swap_seq(): return lax.all_to_all(value, 'seq', split_axis=0, concat_axis=0, tiled=True)  68.4 us
    unnamed x167, local copies, waits for them, and re-layouts  35.1 us
    ppermute x48, starting transfers between devices, swap(): lax.ppermute(value[:, step * lanes:(step + 1) * lanes], 'hid', pairs)  34.6 us
    optimization_barrier x12, local copies, waits for them, and re-layouts, on_device(): lax.optimization_barrier([held[k] for k in names])  33.4 us
  transfers between devices with their start and end apart: 67, of which 41 were waited for; matrix products, arithmetic and copies ran while one was open for 28% of the time, Pallas kernels for 0%

profile of v2, /device:TPU:0, one launch (start us, length us, event | category | flops | bytes accessed | tf_op | source)
XLA Modules:
  0.0 1052.3 jit_solution(393747928747768593)
XLA Ops:
  40.1 9.4 collective-permute-done.1
  49.4 8.8 collective-permute-done.2
  59.8 14.7 %all-to-all-done = bf16[8,16,16,512]{3,2,1,0:T(8,128)(2,1)S(1)} async-done(((bf16[8,16,16,512]{3,2,1,0:T(8,128)(2,1)}), bf16[8,16,16,512]{3,2,1,0:T(8,128)(2,1)S(1)}, u32[]{:S(2)}, u32[]{:S(2)}) %all-to-all-start) | async-done | bytes 2097184 | tf_op jit(solution)/shard_map/all_to_all | solution.py:26
  85.0 12.7 %collective-permute-done.4 = bf16[2048,128]{1,0:T(8,128)(2,1)S(1)} collective-permute-done((bf16[2048,128]{1,0:T(8,128)(2,1)S(1)}, bf16[2048,128]{1,0:T(8,128)(2,1)S(1)}, u32[]{:S(2)}, u32[]{:S(2)}) %collective-permute-start.4) | collective-permute-done | bytes 524320 | tf_op jit(solution)/shard_map/ppermute | solution.py:42
  115.3 11.6 %all-to-all-done.1 = bf16[8,16,16,512]{3,2,1,0:T(8,128)(2,1)} async-done(((bf16[8,16,16,512]{3,2,1,0:T(8,128)(2,1)}), bf16[8,16,16,512]{3,2,1,0:T(8,128)(2,1)}, u32[]{:S(2)}, u32[]{:S(2)}) %all-to-all-start.1) | async-done | bytes 2097184 | tf_op jit(solution)/shard_map/all_to_all | solution.py:26
  136.7 12.7 %collective-permute-done.7 = bf16[2048,128]{1,0:T(8,128)(2,1)S(1)} collective-permute-done((bf16[2048,128]{1,0:T(8,128)(2,1)S(1)}, bf16[2048,128]{1,0:T(8,128)(2,1)S(1)}, u32[]{:S(2)}, u32[]{:S(2)}) %collective-permute-start.7) | collective-permute-done | bytes 524320 | tf_op jit(solution)/shard_map/ppermute | solution.py:42
  149.4 9.0 collective-permute-done.8
  168.5 10.7 %all-to-all-done.2 = bf16[8,16,16,512]{3,2,1,0:T(8,128)(2,1)S(1)} async-done(((bf16[8,16,16,512]{3,2,1,0:T(8,128)(2,1)}), bf16[8,16,16,512]{3,2,1,0:T(8,128)(2,1)S(1)}, u32[]{:S(2)}, u32[]{:S(2)}) %all-to-all-start.2) | async-done | bytes 2097184 | tf_op jit(solution)/shard_map/all_to_all | solution.py:26
  189.9 12.7 %collective-permute-done.10 = bf16[2048,128]{1,0:T(8,128)(2,1)S(1)} collective-permute-done((bf16[2048,128]{1,0:T(8,128)(2,1)S(1)}, bf16[2048,128]{1,0:T(8,128)(2,1)S(1)}, u32[]{:S(2)}, u32[]{:S(2)}) %collective-permute-start.10) | collective-permute-done | bytes 524320 | tf_op jit(solution)/shard_map/ppermute | solution.py:42
  217.5 14.3 %all-to-all-done.3 = bf16[8,16,16,512]{3,2,1,0:T(8,128)(2,1)} async-done(((bf16[8,16,16,512]{3,2,1,0:T(8,128)(2,1)}), bf16[8,16,16,512]{3,2,1,0:T(8,128)(2,1)}, u32[]{:S(2)}, u32[]{:S(2)}) %all-to-all-start.3) | async-done | bytes 2097184 | tf_op jit(solution)/shard_map/all_to_all | solution.py:26
  246.0 42.3 %all-to-all-done.4 = bf16[8,16,16,512]{3,2,1,0:T(8,128)(2,1)} async-done(((bf16[8,16,16,512]{3,2,1,0:T(8,128)(2,1)}), bf16[8,16,16,512]{3,2,1,0:T(8,128)(2,1)}, u32[]{:S(2)}, u32[]{:S(2)}) %all-to-all-start.4) | async-done | bytes 2097184 | tf_op jit(solution)/shard_map/all_to_all | solution.py:26
  385.8 10.6 %collective-permute-done.16 = bf16[2048,128]{1,0:T(8,128)(2,1)S(1)} collective-permute-done((bf16[2048,128]{1,0:T(8,128)(2,1)S(1)}, bf16[2048,128]{1,0:T(8,128)(2,1)S(1)}, u32[]{:S(2)}, u32[]{:S(2)}) %collective-permute-start.16) | collective-permute-done | bytes 524320 | tf_op jit(solution)/shard_map/ppermute | solution.py:42
  448.1 10.5 collective-permute-done.25
  458.6 10.4 collective-permute-done.26
  498.3 8.7 collective-permute-done.29
  508.5 10.1 collective-permute-done.31
  518.6 9.9 collective-permute-done.32
  556.7 8.9 collective-permute-done.35
  567.2 17.8 %all-to-all-done.9 = bf16[8,16,16,512]{3,2,1,0:T(8,128)(2,1)} async-done(((bf16[8,16,16,512]{3,2,1,0:T(8,128)(2,1)}), bf16[8,16,16,512]{3,2,1,0:T(8,128)(2,1)}, u32[]{:S(2)}, u32[]{:S(2)}) %all-to-all-start.9) | async-done | bytes 2097184 | tf_op jit(solution)/shard_map/all_to_all | solution.py:26
  607.8 8.9 collective-permute-done.38
  619.4 18.6 %all-to-all-done.10 = bf16[8,16,16,512]{3,2,1,0:T(8,128)(2,1)} async-done(((bf16[8,16,16,512]{3,2,1,0:T(8,128)(2,1)}), bf16[8,16,16,512]{3,2,1,0:T(8,128)(2,1)}, u32[]{:S(2)}, u32[]{:S(2)}) %all-to-all-start.10) | async-done | bytes 2097184 | tf_op jit(solution)/shard_map/all_to_all | solution.py:26
  660.5 8.4 collective-permute-done.41
  671.6 18.6 %all-to-all-done.11 = bf16[8,16,16,512]{3,2,1,0:T(8,128)(2,1)} async-done(((bf16[8,16,16,512]{3,2,1,0:T(8,128)(2,1)}), bf16[8,16,16,512]{3,2,1,0:T(8,128)(2,1)}, u32[]{:S(2)}, u32[]{:S(2)}) %all-to-all-start.11) | async-done | bytes 2097184 | tf_op jit(solution)/shard_map/all_to_all | solution.py:26
  727.3 18.2 %all-to-all-done.12 = bf16[8,16,16,512]{3,1,2,0:T(8,128)(2,1)} async-done(((bf16[8,16,16,512]{3,1,2,0:T(8,128)(2,1)}), bf16[8,16,16,512]{3,1,2,0:T(8,128)(2,1)}, u32[]{:S(2)}, u32[]{:S(2)}) %all-to-all-start.12) | async-done | bytes 2097184 | tf_op jit(solution)/shard_map/all_to_all | solution.py:26
  770.9 18.7 %collective-permute-done.46 = bf16[2048,128]{1,0:T(8,128)(2,1)S(1)} collective-permute-done((bf16[2048,128]{1,0:T(8,128)(2,1)S(1)}, bf16[2048,128]{1,0:T(8,128)(2,1)S(1)}, u32[]{:S(2)}, u32[]{:S(2)}) %collective-permute-start.46) | collective-permute-done | bytes 524320 | tf_op jit(solution)/shard_map/ppermute | solution.py:42
  789.6 21.2 %collective-permute-done.47 = bf16[2048,128]{1,0:T(8,128)(2,1)S(1)} collective-permute-done((bf16[2048,128]{1,0:T(8,128)(2,1)S(1)}, bf16[2048,128]{1,0:T(8,128)(2,1)S(1)}, u32[]{:S(2)}, u32[]{:S(2)}) %collective-permute-start.47) | collective-permute-done | bytes 524320 | tf_op jit(solution)/shard_map/ppermute | solution.py:42
  826.2 54.2 %all_to_all.80 = bf16[8,16,16,512]{3,1,2,0:T(8,128)(2,1)S(1)} all-to-all(bf16[8,16,16,512]{3,1,2,0:T(8,128)(2,1)S(1)} %copy.134), channel_id=1, replica_groups=mesh['seq'=8,'hid'=4] {'seq'}, dimensions={0} | all-to-all | bytes 4194304 | tf_op jit(solution)/shard_map/all_to_all | solution.py:26
  893.0 51.4 %all_to_all.81 = bf16[8,16,16,512]{3,1,2,0:T(8,128)(2,1)S(1)} all-to-all(bf16[8,16,16,512]{3,1,2,0:T(8,128)(2,1)S(1)} %copy.137), channel_id=1, replica_groups=mesh['seq'=8,'hid'=4] {'seq'}, dimensions={0} | all-to-all | bytes 4194304 | tf_op jit(solution)/shard_map/all_to_all | solution.py:26
  979.0 8.5 copy.135
  992.5 12.7 %fusion.1 = f32[16,512,512]{2,1,0:T(8,128)} fusion(bf16[16,128,512]{2,1,0:T(8,128)(2,1)S(1)} %bitcast.294, bf16[16,128,512]{2,1,0:T(8,128)(2,1)} %bitcast.295, bf16[16,128,512]{2,1,0:T(8,128)(2,1)} %bitcast.297, bf16[16,128,512]{2,1,0:T(8,128)(2,1)} %bitcast.300, bf16[16,128,512]{2,1,0:T(8,128)(2,1)} %bitcast.308, bf16[16,128,512]{2,1,0:T(8,128)(2,1)} %bitcast.306, ...), kind=kOutput, calls=%fused_computation.7 | convolution fusion | flops 4362076160 | bytes 33554432 | tf_op jit(solution)/shard_map/qkj,qkc->qjc/dot_general | solution.py:12
  1005.1 11.4 %fusion = bf16[8192,512]{1,0:T(8,128)(2,1)} fusion(f32[16,8,4,16,512]{4,3,2,1,0:T(8,128)S(1)} %copy.140, f32[16,512,512]{2,1,0:T(8,128)} %fusion.1), kind=kLoop, calls=%fused_computation.4 | loop fusion | flops 8388608 | bytes 41943040 | tf_op jit(solution)/shard_map/convert_element_type | solution.py:222
  1021.7 23.8 %reduce-scatter.14.cloned.1.call-done = f32[64,32,128]{2,1,0:T(8,128)} async-done(((f32[64,128,128]{2,1,0:T(8,128)}), f32[64,32,128]{2,1,0:T(8,128)}) %reduce-scatter.14.cloned.1.call-update) | async-done | bytes 1048592 | tf_op jit(solution)/shard_map/reduce_scatter | solution.py:216
  (407 shorter events, 516.6 us)
Async XLA Ops:
  19.1 55.5 %all-to-all-start = ((bf16[8,16,16,512]{3,2,1,0:T(8,128)(2,1)}), bf16[8,16,16,512]{3,2,1,0:T(8,128)(2,1)S(1)}, u32[]{:S(2)}, u32[]{:S(2)}) async-start(bf16[8,16,16,512]{3,2,1,0:T(8,128)(2,1)} %bitcast.321), calls=%async_computation | async-start | bytes 4194304 | tf_op jit(solution)/shard_map/all_to_all | solution.py:26
  74.6 52.4 %all-to-all-start.1 = ((bf16[8,16,16,512]{3,2,1,0:T(8,128)(2,1)}), bf16[8,16,16,512]{3,2,1,0:T(8,128)(2,1)}, u32[]{:S(2)}, u32[]{:S(2)}) async-start(bf16[8,16,16,512]{3,2,1,0:T(8,128)(2,1)} %bitcast.319), calls=%async_computation.1 | async-start | bytes 4194304 | tf_op jit(solution)/shard_map/all_to_all | solution.py:26
  126.9 52.3 %all-to-all-start.2 = ((bf16[8,16,16,512]{3,2,1,0:T(8,128)(2,1)}), bf16[8,16,16,512]{3,2,1,0:T(8,128)(2,1)S(1)}, u32[]{:S(2)}, u32[]{:S(2)}) async-start(bf16[8,16,16,512]{3,2,1,0:T(8,128)(2,1)} %bitcast.322), calls=%async_computation.2 | async-start | bytes 4194304 | tf_op jit(solution)/shard_map/all_to_all | solution.py:26
  179.2 52.6 %all-to-all-start.3 = ((bf16[8,16,16,512]{3,2,1,0:T(8,128)(2,1)}), bf16[8,16,16,512]{3,2,1,0:T(8,128)(2,1)}, u32[]{:S(2)}, u32[]{:S(2)}) async-start(bf16[8,16,16,512]{3,2,1,0:T(8,128)(2,1)} %bitcast.323), calls=%async_computation.3 | async-start | bytes 4194304 | tf_op jit(solution)/shard_map/all_to_all | solution.py:26
  236.2 52.2 %all-to-all-start.4 = ((bf16[8,16,16,512]{3,2,1,0:T(8,128)(2,1)}), bf16[8,16,16,512]{3,2,1,0:T(8,128)(2,1)}, u32[]{:S(2)}, u32[]{:S(2)}) async-start(bf16[8,16,16,512]{3,2,1,0:T(8,128)(2,1)} %copy.112), calls=%async_computation.4 | async-start | bytes 4194304 | tf_op jit(solution)/shard_map/all_to_all | solution.py:26
  292.5 52.3 %all-to-all-start.5 = ((bf16[8,16,16,512]{3,2,1,0:T(8,128)(2,1)}), bf16[8,16,16,512]{3,2,1,0:T(8,128)(2,1)}, u32[]{:S(2)}, u32[]{:S(2)}) async-start(bf16[8,16,16,512]{3,2,1,0:T(8,128)(2,1)} %copy.114), calls=%async_computation.5 | async-start | bytes 4194304 | tf_op jit(solution)/shard_map/all_to_all | solution.py:26
  349.0 57.4 %all-to-all-start.6 = ((bf16[8,16,16,512]{3,2,1,0:T(8,128)(2,1)}), bf16[8,16,16,512]{3,2,1,0:T(8,128)(2,1)}, u32[]{:S(2)}, u32[]{:S(2)}) async-start(bf16[8,16,16,512]{3,2,1,0:T(8,128)(2,1)} %copy.118), calls=%async_computation.6 | async-start | bytes 4194304 | tf_op jit(solution)/shard_map/all_to_all | solution.py:26
  360.7 23.6 %collective-permute-start.20 = (bf16[2048,128]{1,0:T(8,128)(2,1)S(1)}, bf16[2048,128]{1,0:T(8,128)(2,1)S(1)}, u32[]{:S(2)}, u32[]{:S(2)}) collective-permute-start(bf16[2048,128]{1,0:T(8,128)(2,1)S(1)} %get-tuple-element.537), channel_id=1, source_target_pairs={{0,3},{1,2},{2,1},{3,0},{4,7},{5,6},{6,5},{7,4},{8,11},{9,10},{10,... | collective-permute-start | bytes 1572872 | tf_op jit(solution)/shard_map/ppermute | solution.py:42
  364.4 32.0 %collective-permute-start.16 = (bf16[2048,128]{1,0:T(8,128)(2,1)S(1)}, bf16[2048,128]{1,0:T(8,128)(2,1)S(1)}, u32[]{:S(2)}, u32[]{:S(2)}) collective-permute-start(bf16[2048,128]{1,0:T(8,128)(2,1)S(1)} %get-tuple-element.539), channel_id=1, source_target_pairs={{0,2},{1,3},{2,0},{3,1},{4,6},{5,7},{6,4},{7,5},{8,10},{9,11},{10,... | collective-permute-start | bytes 1572872 | tf_op jit(solution)/shard_map/ppermute | solution.py:42
  366.0 30.4 %collective-permute-start.15 = (bf16[2048,128]{1,0:T(8,128)(2,1)S(1)}, bf16[2048,128]{1,0:T(8,128)(2,1)S(1)}, u32[]{:S(2)}, u32[]{:S(2)}) collective-permute-start(bf16[2048,128]{1,0:T(8,128)(2,1)S(1)} %get-tuple-element.540), channel_id=1, source_target_pairs={{0,1},{1,0},{2,3},{3,2},{4,5},{5,4},{6,7},{7,6},{8,9},{9,8},{10,11... | collective-permute-start | bytes 1572872 | tf_op jit(solution)/shard_map/ppermute | solution.py:42
  374.0 30.8 %collective-permute-start.17 = (bf16[2048,128]{1,0:T(8,128)(2,1)S(1)}, bf16[2048,128]{1,0:T(8,128)(2,1)S(1)}, u32[]{:S(2)}, u32[]{:S(2)}) collective-permute-start(bf16[2048,128]{1,0:T(8,128)(2,1)S(1)} %get-tuple-element.541), channel_id=1, source_target_pairs={{0,3},{1,2},{2,1},{3,0},{4,7},{5,6},{6,5},{7,4},{8,11},{9,10},{10,... | collective-permute-start | bytes 1572872 | tf_op jit(solution)/shard_map/ppermute | solution.py:42
  410.5 60.1 %all-to-all-start.7 = ((bf16[8,16,16,512]{3,2,1,0:T(8,128)(2,1)}), bf16[8,16,16,512]{3,2,1,0:T(8,128)(2,1)}, u32[]{:S(2)}, u32[]{:S(2)}) async-start(bf16[8,16,16,512]{3,2,1,0:T(8,128)(2,1)} %copy.120), calls=%async_computation.7 | async-start | bytes 4194304 | tf_op jit(solution)/shard_map/all_to_all | solution.py:26
  432.4 26.1 %collective-permute-start.25 = (bf16[2048,128]{1,0:T(8,128)(2,1)S(1)}, bf16[2048,128]{1,0:T(8,128)(2,1)S(1)}, u32[]{:S(2)}, u32[]{:S(2)}) collective-permute-start(bf16[2048,128]{1,0:T(8,128)(2,1)S(1)} %get-tuple-element.527), channel_id=1, source_target_pairs={{0,2},{1,3},{2,0},{3,1},{4,6},{5,7},{6,4},{7,5},{8,10},{9,11},{10,... | collective-permute-start | bytes 1572872 | tf_op jit(solution)/shard_map/ppermute | solution.py:42
  433.7 24.8 %collective-permute-start.24 = (bf16[2048,128]{1,0:T(8,128)(2,1)S(1)}, bf16[2048,128]{1,0:T(8,128)(2,1)S(1)}, u32[]{:S(2)}, u32[]{:S(2)}) collective-permute-start(bf16[2048,128]{1,0:T(8,128)(2,1)S(1)} %get-tuple-element.528), channel_id=1, source_target_pairs={{0,1},{1,0},{2,3},{3,2},{4,5},{5,4},{6,7},{7,6},{8,9},{9,8},{10,11... | collective-permute-start | bytes 1572872 | tf_op jit(solution)/shard_map/ppermute | solution.py:42
  436.1 32.9 %collective-permute-start.26 = (bf16[2048,128]{1,0:T(8,128)(2,1)S(1)}, bf16[2048,128]{1,0:T(8,128)(2,1)S(1)}, u32[]{:S(2)}, u32[]{:S(2)}) collective-permute-start(bf16[2048,128]{1,0:T(8,128)(2,1)S(1)} %get-tuple-element.529), channel_id=1, source_target_pairs={{0,3},{1,2},{2,1},{3,0},{4,7},{5,6},{6,5},{7,4},{8,11},{9,10},{10,... | collective-permute-start | bytes 1572872 | tf_op jit(solution)/shard_map/ppermute | solution.py:42
  470.6 59.5 %all-to-all-start.8 = ((bf16[8,16,16,512]{3,2,1,0:T(8,128)(2,1)}), bf16[8,16,16,512]{3,2,1,0:T(8,128)(2,1)}, u32[]{:S(2)}, u32[]{:S(2)}) async-start(bf16[8,16,16,512]{3,2,1,0:T(8,128)(2,1)} %bitcast.347), calls=%async_computation.8 | async-start | bytes 4194304 | tf_op jit(solution)/shard_map/all_to_all | solution.py:26
  483.4 23.6 %collective-permute-start.29 = (bf16[2048,128]{1,0:T(8,128)(2,1)S(1)}, bf16[2048,128]{1,0:T(8,128)(2,1)S(1)}, u32[]{:S(2)}, u32[]{:S(2)}) collective-permute-start(bf16[2048,128]{1,0:T(8,128)(2,1)S(1)} %get-tuple-element.525), channel_id=1, source_target_pairs={{0,3},{1,2},{2,1},{3,0},{4,7},{5,6},{6,5},{7,4},{8,11},{9,10},{10,... | collective-permute-start | bytes 1572872 | tf_op jit(solution)/shard_map/ppermute | solution.py:42
  492.5 26.1 %collective-permute-start.31 = (bf16[2048,128]{1,0:T(8,128)(2,1)S(1)}, bf16[2048,128]{1,0:T(8,128)(2,1)S(1)}, u32[]{:S(2)}, u32[]{:S(2)}) collective-permute-start(bf16[2048,128]{1,0:T(8,128)(2,1)S(1)} %get-tuple-element.519), channel_id=1, source_target_pairs={{0,2},{1,3},{2,0},{3,1},{4,6},{5,7},{6,4},{7,5},{8,10},{9,11},{10,... | collective-permute-start | bytes 1572872 | tf_op jit(solution)/shard_map/ppermute | solution.py:42
  494.5 24.1 %collective-permute-start.30 = (bf16[2048,128]{1,0:T(8,128)(2,1)S(1)}, bf16[2048,128]{1,0:T(8,128)(2,1)S(1)}, u32[]{:S(2)}, u32[]{:S(2)}) collective-permute-start(bf16[2048,128]{1,0:T(8,128)(2,1)S(1)} %get-tuple-element.520), channel_id=1, source_target_pairs={{0,1},{1,0},{2,3},{3,2},{4,5},{5,4},{6,7},{7,6},{8,9},{9,8},{10,11... | collective-permute-start | bytes 1572872 | tf_op jit(solution)/shard_map/ppermute | solution.py:42
  496.2 32.4 %collective-permute-start.32 = (bf16[2048,128]{1,0:T(8,128)(2,1)S(1)}, bf16[2048,128]{1,0:T(8,128)(2,1)S(1)}, u32[]{:S(2)}, u32[]{:S(2)}) collective-permute-start(bf16[2048,128]{1,0:T(8,128)(2,1)S(1)} %get-tuple-element.521), channel_id=1, source_target_pairs={{0,3},{1,2},{2,1},{3,0},{4,7},{5,6},{6,5},{7,4},{8,11},{9,10},{10,... | collective-permute-start | bytes 1572872 | tf_op jit(solution)/shard_map/ppermute | solution.py:42
  530.1 54.9 %all-to-all-start.9 = ((bf16[8,16,16,512]{3,2,1,0:T(8,128)(2,1)}), bf16[8,16,16,512]{3,2,1,0:T(8,128)(2,1)}, u32[]{:S(2)}, u32[]{:S(2)}) async-start(bf16[8,16,16,512]{3,2,1,0:T(8,128)(2,1)} %bitcast.348), calls=%async_computation.9 | async-start | bytes 4194304 | tf_op jit(solution)/shard_map/all_to_all | solution.py:26
  541.9 23.7 %collective-permute-start.35 = (bf16[2048,128]{1,0:T(8,128)(2,1)S(1)}, bf16[2048,128]{1,0:T(8,128)(2,1)S(1)}, u32[]{:S(2)}, u32[]{:S(2)}) collective-permute-start(bf16[2048,128]{1,0:T(8,128)(2,1)S(1)} %get-tuple-element.517), channel_id=1, source_target_pairs={{0,3},{1,2},{2,1},{3,0},{4,7},{5,6},{6,5},{7,4},{8,11},{9,10},{10,... | collective-permute-start | bytes 1572872 | tf_op jit(solution)/shard_map/ppermute | solution.py:42
  585.0 53.0 %all-to-all-start.10 = ((bf16[8,16,16,512]{3,2,1,0:T(8,128)(2,1)}), bf16[8,16,16,512]{3,2,1,0:T(8,128)(2,1)}, u32[]{:S(2)}, u32[]{:S(2)}) async-start(bf16[8,16,16,512]{3,2,1,0:T(8,128)(2,1)} %bitcast.349), calls=%async_computation.10 | async-start | bytes 4194304 | tf_op jit(solution)/shard_map/all_to_all | solution.py:26
  638.0 52.2 %all-to-all-start.11 = ((bf16[8,16,16,512]{3,2,1,0:T(8,128)(2,1)}), bf16[8,16,16,512]{3,2,1,0:T(8,128)(2,1)}, u32[]{:S(2)}, u32[]{:S(2)}) async-start(bf16[8,16,16,512]{3,2,1,0:T(8,128)(2,1)} %bitcast.350), calls=%async_computation.11 | async-start | bytes 4194304 | tf_op jit(solution)/shard_map/all_to_all | solution.py:26
  693.4 52.2 %all-to-all-start.12 = ((bf16[8,16,16,512]{3,1,2,0:T(8,128)(2,1)}), bf16[8,16,16,512]{3,1,2,0:T(8,128)(2,1)}, u32[]{:S(2)}, u32[]{:S(2)}) async-start(bf16[8,16,16,512]{3,1,2,0:T(8,128)(2,1)} %copy.130), calls=%async_computation.12 | async-start | bytes 4194304 | tf_op jit(solution)/shard_map/all_to_all | solution.py:26
  697.7 318.8 %reduce-scatter.6.cloned.1.call-start = ((), (), s32[]{:S(2)}) async-start(), calls=%async_computation.21 | async-start | bytes 5242880 | tf_op jit(solution)/shard_map/reduce_scatter | solution.py:157
  761.0 52.4 %all-to-all-start.13 = ((bf16[8,16,16,512]{3,1,2,0:T(8,128)(2,1)}), bf16[8,16,16,512]{3,1,2,0:T(8,128)(2,1)S(1)}, u32[]{:S(2)}, u32[]{:S(2)}) async-start(bf16[8,16,16,512]{3,1,2,0:T(8,128)(2,1)} %copy.132), calls=%async_computation.13 | async-start | bytes 4194304 | tf_op jit(solution)/shard_map/all_to_all | solution.py:26
  764.7 251.9 %reduce-scatter.8.cloned.1.call-start = ((), (), s32[]{:S(2)}) async-start(), calls=%async_computation.22 | async-start | bytes 5242880 | tf_op jit(solution)/shard_map/reduce_scatter | solution.py:157
  770.3 40.5 %collective-permute-start.47 = (bf16[2048,128]{1,0:T(8,128)(2,1)S(1)}, bf16[2048,128]{1,0:T(8,128)(2,1)S(1)}, u32[]{:S(2)}, u32[]{:S(2)}) collective-permute-start(bf16[2048,128]{1,0:T(8,128)(2,1)S(1)} %get-tuple-element.501), channel_id=1, source_target_pairs={{0,3},{1,2},{2,1},{3,0},{4,7},{5,6},{6,5},{7,4},{8,11},{9,10},{10,... | collective-permute-start | bytes 1572872 | tf_op jit(solution)/shard_map/ppermute | solution.py:42
  824.4 192.1 %reduce-scatter.10.cloned.1.call-start = ((), (), s32[]{:S(2)}) async-start(), calls=%async_computation.23 | async-start | bytes 5242880 | tf_op jit(solution)/shard_map/reduce_scatter | solution.py:157
  891.2 125.3 %reduce-scatter.12.cloned.1.call-start = ((), (), s32[]{:S(2)}) async-start(), calls=%async_computation.24 | async-start | bytes 5242880 | tf_op jit(solution)/shard_map/reduce_scatter | solution.py:157
  955.1 90.4 %reduce-scatter.14.cloned.1.call-start = ((), (), s32[]{:S(2)}) async-start(), calls=%async_computation.25 | async-start | bytes 5242880 | tf_op jit(solution)/shard_map/reduce_scatter | solution.py:216
  (114 other events, 1664.0 us)
Sparse Core Ops, SparseCore 0:
  758.0 59.3 reduce-scatter.5
  824.5 46.5 reduce-scatter.7
  891.3 42.6 reduce-scatter.9
  955.3 42.7 reduce-scatter.11
  1001.0 44.4 reduce-scatter.13
